TPU v7x, 128 devices: a whole 4x4x4 slice. The times are simulated.
128 devices in a mesh: rep: 4 (over y), shard: 16 (over z, x_lo, core), tp: 2 (over x_hi).
Axes of the slice: x: 4 (x_hi: 2, x_lo: 2; x = x_hi * 2 + x_lo), y: 4, z: 4, core: 2. Of those that a mesh axis runs over, the one named last changes fastest.
Arguments:
- hidden_in: bfloat16 [32768, 8192], P(('rep', 'shard', 'tp')), may hold values from -6 to 6
- lengths: int32 [64], P(('rep', 'shard')), may hold values from 128 to 512, as said below
- kv_grad_out: bfloat16 [32768, 2, 1024], P(('rep', 'shard'), None, 'tp'), may hold values from -384 to 384
- master: float32 [8192, 2, 1024], P('shard', None, 'tp'), may hold values from -0.0625 to 0.0625
- moment_one: float32 [8192, 2, 1024], P('shard', None, 'tp'), may hold values from -3 to 3
- moment_two: float32 [8192, 2, 1024], P('shard', None, 'tp'), may hold values from 0.05 to 2
Outputs:
- new_master: float32 [8192, 2, 1024], P('shard', None, 'tp')
- new_moment_one: float32 [8192, 2, 1024], P('shard', None, 'tp')
- new_moment_two: float32 [8192, 2, 1024], P('shard', None, 'tp')
- fresh_kv: bfloat16 [32768, 2, 1024], P(('rep', 'shard'), None, 'tp')
Inputs may be any that keep to these rules, and one draw needn't show every extreme that they name: In block b only its first lengths[b] tokens are valid.
All inputs are finite; a program needn't handle non-finite values.
Results may differ from a plain program's by a relative error of at most 0.014.
Values may be sent and summed in bfloat16 or wider, within the bound.
A program may use at most 192 MiB of HBM per device.

v0:
```python
import jax
import jax.numpy as jnp
from jax import lax
from jax.sharding import PartitionSpec as P

beta_one = 0.9
beta_two = 0.95
step_count = 20
rate = 0.002
decay = 0.1
epsilon = 1e-08


def adamw(master, moment_one, moment_two, grad):
    first = beta_one * moment_one + (1.0 - beta_one) * grad
    second = beta_two * moment_two + (1.0 - beta_two) * grad * grad
    first_hat = first / (1.0 - beta_one**step_count)
    second_hat = second / (1.0 - beta_two**step_count)
    updated = master - rate * (first_hat / (jnp.sqrt(second_hat) + epsilon) + decay * master)
    return (updated, first, second)


def local(hidden_in, lengths, kv_grad_out, master, moment_one, moment_two):
    gathered = lax.all_gather(hidden_in, "tp", axis=0, tiled=True)
    tokens_here = gathered.shape[0]
    features = kv_grad_out.shape[2]
    validity = (jnp.arange(tokens_here, dtype=jnp.int32) < lengths[0]).astype(kv_grad_out.dtype)
    cotan = (kv_grad_out * validity[:, None, None]).reshape(tokens_here, 2 * features)
    local_count = jnp.sum(lengths.astype(jnp.float32))
    count = lax.psum(local_count, ("rep", "shard"))
    contract = (((0,), (0,)), ((), ()))
    columns = gathered
    shard_grad = lax.psum_scatter(
        lax.dot_general(columns, cotan, contract, preferred_element_type=jnp.float32).astype(
            jnp.bfloat16
        ),
        "shard",
        scatter_dimension=0,
        tiled=True,
    )
    summed = lax.psum(shard_grad, "rep").astype(jnp.float32)
    grad = summed.reshape(master.shape) / count
    new_master, new_first, new_second = adamw(master, moment_one, moment_two, grad)
    weights = new_master.astype(jnp.bfloat16)
    piece = lax.all_gather(weights, "shard", axis=0, tiled=True)
    columns = gathered
    flat_piece = piece.reshape(piece.shape[0], 2 * features)
    fresh = jnp.dot(columns, flat_piece, preferred_element_type=jnp.float32)
    fresh_kv = fresh.astype(jnp.bfloat16).reshape(tokens_here, 2, features)
    return (new_master, new_first, new_second, fresh_kv)


def solution(mesh):
    in_specs = (
        P(("rep", "shard", "tp"), None),
        P(("rep", "shard")),
        P(("rep", "shard"), None, "tp"),
        P("shard", None, "tp"),
        P("shard", None, "tp"),
        P("shard", None, "tp"),
    )
    out_specs = (
        P("shard", None, "tp"),
        P("shard", None, "tp"),
        P("shard", None, "tp"),
        P(("rep", "shard"), None, "tp"),
    )
    return jax.shard_map(local, mesh=mesh, in_specs=in_specs, out_specs=out_specs, check_vma=False)
```

profile of v0, /device:TPU:1, one launch (start us, length us, event | category | flops | bytes accessed | tf_op | source)
XLA Modules:
  0.0 603.2 jit_solution(5679530986806273875)
XLA Ops:
  7.2 0.0 copy-start.1
  7.2 0.0 all-gather.3.cloned.1.call-start
  7.2 0.7 all-gather.3.cloned.1.call-update
  7.9 0.0 reduce-scatter.2.cloned.1.call-start
  8.6 0.0 copy-done.1
  8.6 1.8 broadcast_multiply_fusion
  10.5 0.2 copy.39
  10.7 110.2 %all-gather.3.cloned.1.call-done = bf16[512,8192]{1,0:T(8,128)(2,1)} async-done(((bf16[256,8192]{1,0:T(8,128)(2,1)}), bf16[512,8192]{1,0:T(8,128)(2,1)}) %all-gather.3.cloned.1.call-update) | async-done | bytes 8388624 | tf_op jit(solution)/shard_map/all_gather | solution.py:24
  120.9 15.8 %convert_bitcast_fusion = bf16[8192,1024]{0,1:T(8,128)(2,1)} fusion(bf16[512,1024]{1,0:T(8,128)(2,1)S(1)} %bitcast.21, bf16[512,8192]{1,0:T(8,128)(2,1)} %all-gather.3.cloned.1.call-done), kind=kOutput, calls=%fused_computation | convolution fusion | flops 8598323200 | bytes 26214400 | tf_op jit(solution)/shard_map/dot_general | solution.py:34
  136.7 0.0 reduce-scatter.2.cloned.1.call-update
  136.7 0.0 all-reduce.2.cloned.1.call-start
  136.8 180.2 %reduce-scatter.2.cloned.1.call-done = bf16[512,1024]{0,1:T(8,128)(2,1)} async-done(((bf16[8192,1024]{0,1:T(8,128)(2,1)}), bf16[512,1024]{0,1:T(8,128)(2,1)}) %reduce-scatter.2.cloned.1.call-update) | async-done | bytes 1048592 | tf_op jit(solution)/shard_map/reduce_scatter | solution.py:33
  317.0 0.0 all-reduce.2.cloned.1.call-update
  317.0 0.0 all-gather.5.cloned.1.call-start
  317.0 142.0 %psum.15 = f32[]{:T(128)} all-reduce(f32[]{:T(128)} %bitcast.2), channel_id=1, replica_groups=mesh['rep'=4,'shard'=16,'tp'=2] {'rep','shard'}, use_global_device_ids=true, to_apply=%region_2.0 | all-reduce | flops 1 | bytes 8 | tf_op jit(solution)/shard_map/psum | solution.py:30
  459.0 0.0 all-reduce.2.cloned.1.call-done
  459.0 2.2 convert_divide_fusion
  461.2 1.8 copy.28
  463.0 7.5 %fusion.3 = (bf16[512,2,512]{2,0,1:T(8,128)(2,1)S(1)}, f32[512,2,512]{2,0,1:T(8,128)}, f32[512,2,512]{2,0,1:T(8,128)}, f32[512,2,512]{2,0,1:T(8,128)S(1)}) fusion(f32[512,2,512]{2,1,0:T(2,128)} %param.9, f32[512,2,512]{2,0,1:T(8,128)} %copy.28, f32[512,2,512]{2,1,0:T(2,128)} %param.10, f32[512,2,512]{2,1,0:T(2,128)} %param.11), kind=kLoop, calls=%fused_computation.12 | loop fusion | flops 8388608 | bytes 15728640 | tf_op jit(solution)/shard_map/convert_element_type | solution.py:44
  470.5 2.0 copy.34
  472.6 0.0 all-gather.5.cloned.1.call-update
  472.6 0.0 copy-start
  472.6 4.7 copy.35
  477.3 0.0 copy-done
  477.3 2.9 copy.36
  480.2 2.9 copy.37
  483.2 79.9 %all-gather.5.cloned.1.call-done = bf16[8192,2,512]{2,1,0:T(2,128)(2,1)} async-done(((bf16[512,2,512]{2,1,0:T(2,128)(2,1)}), bf16[8192,2,512]{2,1,0:T(2,128)(2,1)}) %all-gather.5.cloned.1.call-update) | async-done | bytes 16777232 | tf_op jit(solution)/shard_map/all_gather | solution.py:45
  563.0 16.6 %copy.40 = bf16[1024,8,2,512]{3,1,2,0:T(8,128)(2,1)} copy(bf16[1024,8,2,512]{3,2,1,0:T(2,128)(2,1)} %bitcast.17) | data formatting | bytes 33554432
  579.6 14.9 %convolution_convert_fusion = bf16[1024,512]{1,0:T(8,128)(2,1)S(1)} fusion(bf16[8192,1024]{1,0:T(8,128)(2,1)} %bitcast.18, bf16[512,8192]{1,0:T(8,128)(2,1)} %all-gather.3.cloned.1.call-done), kind=kOutput, calls=%fused_computation.8 | convolution fusion | flops 8590458880 | bytes 26214400 | tf_op jit(solution)/shard_map/dot_general | solution.py:48
  594.5 2.1 copy.38
  (1 shorter events, 0.0 us)
Async XLA Ops:
  7.2 1.5 copy-start.1
  7.2 113.8 %all-gather.3.cloned.1.call-start = ((), (), s32[]{:S(2)}) async-start(), calls=%async_computation.1 | async-start | bytes 12582912 | tf_op jit(solution)/shard_map/all_gather | solution.py:24
  7.9 309.1 %reduce-scatter.2.cloned.1.call-start = ((), (), s32[]{:S(2)}) async-start(), calls=%async_computation.2 | async-start | bytes 17825792 | tf_op jit(solution)/shard_map/reduce_scatter | solution.py:33
  136.7 322.3 %all-reduce.2.cloned.1.call-start = ((), (), s32[]{:S(2)}) async-start(), calls=%async_computation.3 | async-start | bytes 2097152 | tf_op jit(solution)/shard_map/psum | solution.py:41
  317.0 246.0 %all-gather.5.cloned.1.call-start = ((), (), s32[]{:S(2)}) async-start(), calls=%async_computation.4 | async-start | bytes 17825792 | tf_op jit(solution)/shard_map/all_gather | solution.py:45
  472.6 4.7 copy-start
Sparse Core Ops, SparseCore 0:
  9.7 111.2 all-gather.2
  136.8 180.0 reduce-scatter.1
  319.3 45.2 all-reduce.1
  472.7 90.2 all-gather.4
where the time goes:
time: 603 us
  waiting for transfers between devices  371 us (62%)
  blocking collectives  142 us (24%)
  local copies, waits for them, and re-layouts  33.3 us (6%)
  matrix products  30.6 us (5%)
  between operations  14.5 us (2%)
  other arithmetic  11.5 us (2%)
    reduce_scatter x1, waiting for transfers between devices, local(): lax.psum_scatter(lax.dot_general(columns, cotan, contract, preferred_elem...  180 us
    psum x1, blocking collectives, local(): count = lax.psum(local_count, ('rep', 'shard'))  142 us
    all_gather x1, waiting for transfers between devices, local(): gathered = lax.all_gather(hidden_in, 'tp', axis=0, tiled=True)  110 us
    all_gather x1, waiting for transfers between devices, local(): piece = lax.all_gather(weights, 'shard', axis=0, tiled=True)  79.9 us
    unnamed x10, local copies, waits for them, and re-layouts  29.5 us
    dot_general x1, matrix products, local(): lax.dot_general(columns, cotan, contract, preferred_element_type=jnp.floa...  15.8 us
    dot_general x1, matrix products, local(): fresh = jnp.dot(columns, flat_piece, preferred_element_type=jnp.float32)  14.9 us
  transfers between devices with their start and end apart: 4, of which 3 were waited for; matrix products, arithmetic and copies ran while one was open for 2% of the time, Pallas kernels for 0%

commit v1 on v0

v1 whole, which is shorter than its diff:
```python
import functools

import jax
import jax.numpy as jnp
from jax import lax
from jax.experimental import pallas as pl
from jax.experimental.pallas import tpu as pltpu
from jax.sharding import PartitionSpec as P

MESH = pl.DeviceIdType.MESH
F32, BF16 = jnp.float32, jnp.bfloat16

beta_one = 0.9
beta_two = 0.95
step_count = 20
rate = 0.002
decay = 0.1
epsilon = 1e-08

NJ = 4
TOK = 512
FEAT = 1024
HALF = 512


def adamw(master, moment_one, moment_two, grad):
    first = beta_one * moment_one + (1.0 - beta_one) * grad
    second = beta_two * moment_two + (1.0 - beta_two) * grad * grad
    first_hat = first / (1.0 - beta_one**step_count)
    second_hat = second / (1.0 - beta_two**step_count)
    updated = master - rate * (first_hat / (jnp.sqrt(second_hat) + epsilon) + decay * master)
    return (updated, first, second)


def main_kernel(
    hid,
    lengths,
    kv,
    master,
    first,
    second,
    fresh_out,
    g_out,
    count_out,
    hbuf,
    cbuf,
    kvbuf,
    gbuf,
    r1,
    r2a,
    r2b,
    r3,
    r4,
    wbuf,
    acc,
    fsend,
    frecv,
    mbuf,
    cnt,
    send_s,
    recv_s,
    gg_s,
    gg_r,
    h_s,
    h_r,
    h_l,
    small_s,
    small_r,
    load_s,
):
    y = lax.axis_index("rep")
    s = lax.axis_index("shard")
    t = lax.axis_index("tp")
    z = s // 4
    xl = (s // 2) % 2
    c = s % 2

    def ydev(d):
        return ((y + d) % 4, s, t)

    def zdev(d):
        return (y, ((z + d) % 4) * 4 + s % 4, t)

    xdev = (y, z * 4 + (1 - xl) * 2 + c, t)
    sib = (y, z * 4 + xl * 2 + (1 - c), t)

    def partner(core):
        return (y, z * 4 + xl * 2 + core, 1 - t)

    peers = [ydev(1), ydev(2), ydev(3), zdev(1), zdev(2), zdev(3), xdev, sib, partner(0), partner(1)]
    sends = []

    def put(src, dst, ss, rs, dev):
        copy = pltpu.make_async_remote_copy(src, dst, ss, rs, device_id=dev, device_id_type=MESH)
        copy.start()
        sends.append(copy)

    def got(dst, rs):
        pltpu.make_async_remote_copy(dst, dst, rs, rs, device_id=sib, device_id_type=MESH).wait_recv()

    kv_load = pltpu.make_async_copy(kv, kvbuf, load_s.at[3])
    kv_load.start()
    loads = []
    for k, ref in enumerate((master, first, second)):
        for j in range(NJ):
            loads.append(
                pltpu.make_async_copy(
                    ref.at[pl.ds(j * 128 + y * 32, 32)], mbuf.at[k, j], load_s.at[4 + k * NJ + j]
                )
            )
    for load in loads:
        load.start()

    mine = pl.ds(pl.multiple_of(c * 512 + t * 256, 256), 256)

    def columns(j, q, core):
        return pl.ds(pl.multiple_of((2 * q + core) * 512 + j * 128, 128), 128)

    def h_local(j):
        @pl.loop(0, 8)
        def _(q):
            pltpu.make_async_copy(
                hid.at[:, columns(j, q, c)],
                hbuf.at[j, mine, pl.ds(pl.multiple_of(q * 128, 128), 128)],
                h_l.at[j],
            ).start()

    def h_send(j):
        for k, (dev, core) in enumerate(((partner(0), 0), (partner(1), 1), (sib, 1 - c))):

            @pl.loop(0, 8)
            def _(q):
                pltpu.make_async_remote_copy(
                    hid.at[:, columns(j, q, core)],
                    hbuf.at[j, mine, pl.ds(pl.multiple_of(q * 128, 128), 128)],
                    h_s.at[j, k],
                    h_r.at[j, c * 2 + t],
                    device_id=dev,
                    device_id_type=MESH,
                ).start()

    def h_wait(j):
        pltpu.make_async_copy(hbuf.at[j, mine], hbuf.at[j, mine], h_l.at[j]).wait()
        for core, tp in ((1 - c, t), (0, 1 - t), (1, 1 - t)):
            rows = pl.ds(pl.multiple_of(core * 512 + tp * 256, 256), 256)
            got(hbuf.at[j, rows], h_r.at[j, core * 2 + tp])

    for j in range(NJ):
        h_local(j)

    barrier = pltpu.get_barrier_semaphore()
    for dev in peers:
        pl.semaphore_signal(barrier, inc=1, device_id=dev, device_id_type=MESH)
    pl.semaphore_wait(barrier, len(peers))

    h_send(0)
    h_send(1)

    def count_step(base, n, me, devs, sem):
        for d in range(1, n):
            put(cnt.at[base + me], cnt.at[base + me], small_s.at[sem + d], small_r.at[sem + d], devs(d))

    def count_sum(base, n, me, sem):
        for d in range(1, n):
            got(cnt.at[base + (me + n - d) % n], small_r.at[sem + d])
        total = cnt[base]
        for d in range(1, n):
            total = total + cnt[base + d]
        return total

    cnt[y] = jnp.full((8, 128), lengths[0], jnp.int32).astype(F32)
    count_step(0, 4, y, ydev, 0)

    kv_load.wait()

    @pl.loop(0, 8)
    def _(b):
        rows = pl.ds(pl.multiple_of(b * 64, 64), 64)
        value = kvbuf[rows].astype(F32)
        token = lax.broadcasted_iota(jnp.int32, (64, 8, 128), 0) + b * 64
        value = jnp.where(token < lengths[0], value, 0.0)
        cbuf[pl.ds(pl.multiple_of(c * 512 + b * 64, 64), 64)] = value.reshape(64, FEAT).astype(BF16)

    own_c = cbuf.at[pl.ds(pl.multiple_of(c * 512, 512), 512)]
    sib_c = cbuf.at[pl.ds(pl.multiple_of((1 - c) * 512, 512), 512)]
    put(own_c, own_c, small_s.at[0], small_r.at[0], sib)

    cnt[4 + z] = count_sum(0, 4, y, 0)
    count_step(4, 4, z, zdev, 4)
    cnt[8 + xl] = count_sum(4, 4, z, 4)
    count_step(8, 2, xl, lambda d: xdev, 8)
    cnt[10 + c] = count_sum(8, 2, xl, 8)
    count_step(10, 2, c, lambda d: sib, 10)
    count_out[...] = count_sum(10, 2, c, 10)

    got(sib_c, small_r.at[0])

    index = ((y, z), (z, y))
    devs = ((ydev, zdev), (zdev, ydev))
    r2 = (r2a, r2b)
    every = slice(None)

    def at(h, a1, a2, x=every):
        if h == 0:
            return (a2, x, a1)
        return (a1, x, a2)

    def unit(buf, j, h, a1, a2=every, x=every):
        return buf.at[(j, h) + at(h, a1, a2, x)]

    LOW, HIGH = pl.ds(0, 2), pl.ds(2, 2)

    def g0(j):
        h_wait(j)
        if j + 2 < NJ:
            h_send(j + 2)

        @pl.loop(0, 4)
        def _(zz):
            left = hbuf[j, :, pl.ds(pl.multiple_of(zz * 256, 256), 256)]
            for h in range(2):
                part = lax.dot_general(
                    left,
                    cbuf[:, h * HALF : (h + 1) * HALF],
                    (((0,), (0,)), ((), ())),
                    preferred_element_type=F32,
                )
                gbuf[j, h, zz] = part.astype(BF16).reshape(2, 4, 32, HALF)

        for h in range(2):
            i1 = index[h][0]
            far = (i1 + 2) % 4
            put(unit(gbuf, j, h, far, LOW), r1.at[j, h, 0], send_s.at[j, h, 0], recv_s.at[j, h, 0], devs[h][0](1))
            put(unit(gbuf, j, h, far, HIGH), r1.at[j, h, 1], send_s.at[j, h, 1], recv_s.at[j, h, 1], devs[h][0](3))

    def g1(j):
        for h in range(2):
            i1 = index[h][0]
            for k, (d, low) in enumerate(((1, 0), (3, 2))):
                got(r1.at[j, h, k], recv_s.at[j, h, k])
                to = (i1 + d) % 4
                for a in range(2):
                    for b in range(2):
                        if h == 0:
                            spot = (j, h, low + a, b, to)
                        else:
                            spot = (j, h, to, a, low + b)
                        gbuf[spot] = (gbuf[spot].astype(F32) + r1[j, h, k, a, b].astype(F32)).astype(BF16)
                put(unit(gbuf, j, h, to), r2[h].at[j, k], send_s.at[j, h, 2 + k], recv_s.at[j, h, 2 + k], devs[h][0](d))

    def g2(j):
        for h in range(2):
            i1, i2 = index[h]
            for k in range(2):
                got(r2[h].at[j, k], recv_s.at[j, h, 2 + k])

            @pl.loop(0, 8)
            def _(n):
                a2, x = n // 2, n % 2
                spot = (j, h) + at(h, i1, a2, x)
                here = (a2, x) if h == 0 else (x, a2)
                gbuf[spot] = (
                    gbuf[spot].astype(F32)
                    + r2[h][(j, 0) + here].astype(F32)
                    + r2[h][(j, 1) + here].astype(F32)
                ).astype(BF16)

            for d in range(1, 4):
                put(
                    unit(gbuf, j, h, i1, (i2 + d) % 4),
                    r3.at[j, h, d - 1],
                    send_s.at[j, h, 3 + d],
                    recv_s.at[j, h, 3 + d],
                    devs[h][1](d),
                )

    def g3(j):
        for h in range(2):
            i1, i2 = index[h]
            for d in range(1, 4):
                got(r3.at[j, h, d - 1], recv_s.at[j, h, 3 + d])
            for x in range(2):
                spot = (j, h) + at(h, i1, i2, x)
                total = gbuf[spot].astype(F32)
                for d in range(3):
                    total = total + r3[j, h, d, x].astype(F32)
                gbuf[spot] = total.astype(BF16)
            put(unit(gbuf, j, h, i1, i2, 1 - xl), r4.at[j, h], send_s.at[j, h, 7], recv_s.at[j, h, 7], xdev)

    def g4(j):
        for k in range(3):
            loads[k * NJ + j].wait()
        count = jnp.broadcast_to(count_out[0:1, 0:1], (32, FEAT))
        halves = []
        for h in range(2):
            i1, i2 = index[h]
            got(r4.at[j, h], recv_s.at[j, h, 7])
            halves.append(gbuf[(j, h) + at(h, i1, i2, xl)].astype(F32) + r4[j, h].astype(F32))
        summed = jnp.concatenate(halves, axis=1).astype(BF16)
        g_out[j, y] = summed
        grad = summed.astype(F32) / count
        new, _, _ = adamw(
            mbuf[0, j].reshape(32, FEAT), mbuf[1, j].reshape(32, FEAT), mbuf[2, j].reshape(32, FEAT), grad
        )
        new = new.astype(BF16)
        for h in range(2):
            i1, i2 = index[h]
            wbuf[(j, h) + at(h, i1, i2, xl)] = new[:, h * HALF : (h + 1) * HALF]
            own = unit(wbuf, j, h, i1, i2, xl)
            put(own, own, send_s.at[j, h, 8], recv_s.at[j, h, 8], xdev)
        for d in range(1, 4):
            put(g_out.at[j, y], g_out.at[j, y], gg_s.at[j, d - 1], gg_r.at[j, d - 1], ydev(d))

    def w1(j):
        for h in range(2):
            i1, i2 = index[h]
            got(unit(wbuf, j, h, i1, i2, 1 - xl), recv_s.at[j, h, 8])
            for d in range(1, 4):
                own = unit(wbuf, j, h, i1, i2)
                put(own, own, send_s.at[j, h, 8 + d], recv_s.at[j, h, 8 + d], devs[h][1](d))

    def w2(j):
        for h in range(2):
            i1, i2 = index[h]
            for d in range(1, 4):
                got(unit(wbuf, j, h, i1, (i2 + 4 - d) % 4), recv_s.at[j, h, 8 + d])
            own = unit(wbuf, j, h, i1)
            for k, d in enumerate((1, 3)):
                put(own, own, send_s.at[j, h, 12 + k], recv_s.at[j, h, 12 + k], devs[h][0](d))

    def w3(j):
        for h in range(2):
            i1 = index[h][0]
            for k, (d, part) in enumerate(((1, LOW), (3, HIGH))):
                back = (i1 + 4 - d) % 4
                got(unit(wbuf, j, h, back), recv_s.at[j, h, 12 + k])
                piece = unit(wbuf, j, h, back, part)
                put(piece, piece, send_s.at[j, h, 14 + k], recv_s.at[j, h, 14 + k], devs[h][0](d))

    def w4(j):
        for h in range(2):
            far = (index[h][0] + 2) % 4
            for k, part in enumerate((LOW, HIGH)):
                got(unit(wbuf, j, h, far, part), recv_s.at[j, h, 14 + k])
        if j < NJ - 1:

            @pl.loop(0, 4)
            def _(b):
                rows = pl.ds(pl.multiple_of(b * 256, 256), 256)
                left = hbuf[j, rows]
                for h in range(2):
                    part = jnp.dot(left, wbuf[j, h].reshape(1024, HALF), preferred_element_type=F32)
                    cols = slice(h * HALF, (h + 1) * HALF)
                    if j == 0:
                        acc[rows, cols] = part
                    else:
                        acc[rows, cols] += part
        else:
            for own in range(2):
                core = c if own else 1 - c

                @pl.loop(0, 2)
                def _(b):
                    rows = pl.ds(pl.multiple_of(core * 512 + b * 256, 256), 256)
                    here = pl.ds(pl.multiple_of(b * 256, 256), 256)
                    left = hbuf[j, rows]
                    for h in range(2):
                        part = jnp.dot(left, wbuf[j, h].reshape(1024, HALF), preferred_element_type=F32)
                        cols = slice(h * HALF, (h + 1) * HALF)
                        if own:
                            acc[rows, cols] += part
                        else:
                            fsend[here, cols] = (acc[rows, cols] + part).astype(BF16)

                if not own:
                    put(fsend, frecv, small_s.at[12], small_r.at[12], sib)
            got(frecv, small_r.at[12])

            @pl.loop(0, 4)
            def _(b):
                rows = pl.ds(pl.multiple_of(c * 512 + b * 128, 128), 128)
                here = pl.ds(pl.multiple_of(b * 128, 128), 128)
                fresh_out[here] = (acc[rows] + frecv[here].astype(F32)).astype(BF16)

    g0(0)
    g1(0)
    g2(0)
    g3(0)
    g4(0)
    for j in range(1, NJ):
        w1(j - 1)
        g0(j)
        w2(j - 1)
        g1(j)
        w3(j - 1)
        g2(j)
        w4(j - 1)
        g3(j)
        g4(j)
    w1(NJ - 1)
    w2(NJ - 1)
    w3(NJ - 1)
    w4(NJ - 1)

    for j in range(NJ):
        for d in range(1, 4):
            got(g_out.at[j, (y + 4 - d) % 4], gg_r.at[j, d - 1])
        for k in range(3):
            whole = hbuf.at[j, mine]
            pltpu.make_async_remote_copy(
                whole, whole, h_s.at[j, k], h_s.at[j, k], device_id=sib, device_id_type=MESH
            ).wait_send()
    for copy in sends:
        copy.wait_send()


def finish_kernel(g, count, master, first, second, fresh, new_master, new_first, new_second, fresh_out):
    rows = master.shape[0]
    summed = g[...].astype(F32).reshape(rows, 8, 128)
    grad = summed / jnp.broadcast_to(count[...][0:1, 0:1].reshape(1, 1, 1), (rows, 8, 128))
    a, b, d = adamw(master[...], first[...], second[...], grad)
    new_master[...] = a
    new_first[...] = b
    new_second[...] = d
    fresh_out[...] = fresh[...].astype(F32).reshape(rows, 8, 128).astype(BF16)


def tiles(array):
    n = array.shape[0]
    return array.reshape(n, 2, 4, 128).transpose(0, 2, 1, 3).reshape(n, 8, 128)


def untiles(array):
    n = array.shape[0]
    return array.reshape(n, 4, 2, 128).transpose(0, 2, 1, 3).reshape(n, 2, 512)


def local(hidden_in, lengths, kv_grad_out, master, moment_one, moment_two):
    kv = tiles(kv_grad_out)
    states = [tiles(a) for a in (master, moment_one, moment_two)]
    hbm = pl.BlockSpec(memory_space=pl.ANY)
    vmem = pl.BlockSpec(memory_space=pltpu.VMEM)
    dma = pltpu.SemaphoreType.DMA
    fresh, g, count = pl.pallas_call(
        main_kernel,
        out_shape=(
            jax.ShapeDtypeStruct((TOK, FEAT), BF16),
            jax.ShapeDtypeStruct((NJ, 4, 32, FEAT), BF16),
            jax.ShapeDtypeStruct((8, 128), F32),
        ),
        in_specs=[hbm, pl.BlockSpec(memory_space=pltpu.SMEM), hbm, hbm, hbm, hbm],
        out_specs=(vmem, vmem, vmem),
        scratch_shapes=[
            pltpu.VMEM((NJ, 1024, 1024), BF16),
            pltpu.VMEM((1024, FEAT), BF16),
            pltpu.VMEM((TOK, 8, 128), BF16),
            pltpu.VMEM((NJ, 2, 4, 2, 4, 32, HALF), BF16),
            pltpu.VMEM((NJ, 2, 2, 2, 2, 32, HALF), BF16),
            pltpu.VMEM((NJ, 2, 4, 2, 32, HALF), BF16),
            pltpu.VMEM((NJ, 2, 2, 4, 32, HALF), BF16),
            pltpu.VMEM((NJ, 2, 3, 2, 32, HALF), BF16),
            pltpu.VMEM((NJ, 2, 32, HALF), BF16),
            pltpu.VMEM((NJ, 2, 4, 2, 4, 32, HALF), BF16),
            pltpu.VMEM((1024, FEAT), F32),
            pltpu.VMEM((TOK, FEAT), BF16),
            pltpu.VMEM((TOK, FEAT), BF16),
            pltpu.VMEM((3, NJ, 32, 8, 128), F32),
            pltpu.VMEM((12, 8, 128), F32),
            dma((NJ, 2, 16)),
            dma((NJ, 2, 16)),
            dma((NJ, 3)),
            dma((NJ, 3)),
            dma((NJ, 3)),
            dma((NJ, 4)),
            dma((NJ,)),
            dma((13,)),
            dma((13,)),
            dma((4 + 3 * NJ,)),
        ],
        compiler_params=pltpu.CompilerParams(
            collective_id=0, has_side_effects=True, vmem_limit_bytes=60 * 2**20
        ),
        name="project",
    )(hidden_in, lengths, kv, *states)
    g = g.reshape(TOK, FEAT)
    step = 64
    flat = pl.BlockSpec((step, FEAT), lambda i: (i, 0))
    cube = pl.BlockSpec((step, 8, 128), lambda i: (i, 0, 0))
    outs = pl.pallas_call(
        finish_kernel,
        grid=(TOK // step,),
        out_shape=[jax.ShapeDtypeStruct((TOK, 8, 128), F32)] * 3
        + [jax.ShapeDtypeStruct((TOK, 8, 128), BF16)],
        in_specs=[flat, pl.BlockSpec((8, 128), lambda i: (0, 0)), cube, cube, cube, flat],
        out_specs=[cube] * 4,
        compiler_params=pltpu.CompilerParams(vmem_limit_bytes=32 * 2**20),
        name="update",
    )(g, count, *states, fresh)
    return tuple(untiles(a) for a in outs)


def solution(mesh):
    in_specs = (
        P(("rep", "shard", "tp"), None),
        P(("rep", "shard")),
        P(("rep", "shard"), None, "tp"),
        P("shard", None, "tp"),
        P("shard", None, "tp"),
        P("shard", None, "tp"),
    )
    out_specs = (
        P("shard", None, "tp"),
        P("shard", None, "tp"),
        P("shard", None, "tp"),
        P(("rep", "shard"), None, "tp"),
    )
    return jax.shard_map(local, mesh=mesh, in_specs=in_specs, out_specs=out_specs, check_vma=False)
```

time: 603 us -> 219 us (0.36)
  waiting for transfers between devices: 371 us -> 0 us
  Pallas kernels: 0 us -> 212 us
  blocking collectives: 142 us -> 0 us
  matrix products: 30.6 us -> 0 us
  local copies, waits for them, and re-layouts: 33.3 us -> 6.31 us
  between operations: 14.5 us -> 1.31 us
  other arithmetic: 11.5 us -> 0 us
    pallas_call x0 -> x2, Pallas kernels: none -> 212 us  [the longest x1 206 us: local(): pl.pallas_call(main_kernel, out_shape=(jax.ShapeDtypeStruct((TOK, FEAT),...]
    all_gather x2 -> x0, waiting for transfers between devices: 190 us -> none  [the longest x1 110 us: local(): gathered = lax.all_gather(hidden_in, 'tp', axis=0, tiled=True)]
    reduce_scatter x1 -> x0, waiting for transfers between devices: 180 us -> none  [local(): lax.psum_scatter(lax.dot_general(columns, cotan, contract, preferred_elem...]
    psum x1 -> x0, blocking collectives: 142 us -> none  [local(): count = lax.psum(local_count, ('rep', 'shard'))]
    dot_general x2 -> x0, matrix products: 30.6 us -> none  [the longest x1 15.8 us: local(): lax.dot_general(columns, cotan, contract, preferred_element_type=jnp.floa...]
    unnamed x10 -> x12, local copies, waits for them, and re-layouts: 29.5 us -> 6.31 us
    convert_element_type x2 -> x0, other arithmetic: 7.54 us -> none  [the longest x1 7.53 us: local(): weights = new_master.astype(jnp.bfloat16)]
  transfers between devices with their start and end apart: 4 -> 0, of which waited for: 3 -> 0; matrix products, arithmetic and copies ran while one was open for 2% -> 0% of each run, Pallas kernels for 0% -> 0%
where the time goes in v1:
time: 219 us
  Pallas kernels  212 us (97%)
  local copies, waits for them, and re-layouts  6.31 us (3%)
    pallas_call x1, Pallas kernels, local(): pl.pallas_call(main_kernel, out_shape=(jax.ShapeDtypeStruct((TOK, FEAT),...  206 us
    unnamed x12, local copies, waits for them, and re-layouts  6.31 us
    pallas_call x1, Pallas kernels, local(): pl.pallas_call(finish_kernel, grid=(TOK // step,), out_shape=[jax.ShapeDt...  5.22 us

profile of v1, /device:TPU:1, one launch (start us, length us, event | category | flops | bytes accessed | tf_op | source)
XLA Modules:
  0.0 219.2 jit_solution(2107136049640776014)
XLA Ops:
  1.3 0.0 copy-start
  1.3 206.3 %project.1 = (bf16[512,1024]{1,0:T(8,128)(2,1)}, bf16[4,4,32,1024]{3,2,1,0:T(8,128)(2,1)}, f32[8,128]{1,0:T(8,128)}) custom-call(bf16[256,8192]{1,0:T(8,128)(2,1)} %hid.1, s32[1]{0:T(128)S(6)} %copy.18.lengths, bf16[512,8,128]{2,1,0:T(8,128)(2,1)} %bitcast.48, f32[512,8,128]{2,1,0:T(8,128)} %bitcast.41, f32[512,8,128]{2,1,0:T(8,128)} %bitcast.43, ...), custom_call_target="tpu_custom_call" | custom-call | tf_op jit(solution)/shard_map/project/pallas_call | solution.py:444
  207.6 0.0 copy-done
  207.6 0.0 copy-start.1
  207.6 1.6 copy-done.1
  209.2 0.0 copy-start.2
  209.2 1.6 copy-done.2
  210.8 0.0 copy-start.3
  210.8 1.2 copy-done.3
  212.0 0.0 copy-start.4
  212.0 1.2 copy-done.4
  213.3 0.0 copy-start.5
  213.3 0.7 copy-done.5
  214.0 5.2 %update.1 = (f32[512,8,128]{2,1,0:T(8,128)}, f32[512,8,128]{2,1,0:T(8,128)}, f32[512,8,128]{2,1,0:T(8,128)}, bf16[512,8,128]{2,1,0:T(8,128)(2,1)}) custom-call(bf16[512,1024]{1,0:T(8,128)(2,1)S(1)} %bitcast.47, f32[8,128]{1,0:T(8,128)S(1)} %copy-done.5, f32[512,8,128]{2,1,0:T(8,128)S(1)} %bitcast.42, f32[512,8,128]{2,1,0:T(8,128)S(1)} %bitcast.44, ...), custom_call_target="tpu_custom_call" | custom-call | tf_op jit(solution)/shard_map/update/pallas_call | solution.py:489
Async XLA Ops:
  1.3 206.3 %copy-start = (f32[512,2,512]{2,1,0:T(2,128)S(1)}, f32[512,2,512]{2,1,0:T(2,128)}, u32[]{:S(2)}) copy-start(f32[512,2,512]{2,1,0:T(2,128)} %param.9) | copy-start | bytes 6291460
  207.6 1.6 copy-start.1
  209.2 1.6 copy-start.2
  210.8 1.2 copy-start.3
  212.0 1.2 copy-start.4
  213.3 0.7 copy-start.5

commit v2 on v1

v2 whole, which is shorter than its diff:
```python
import functools

import jax
import jax.numpy as jnp
from jax import lax
from jax.experimental import pallas as pl
from jax.experimental.pallas import tpu as pltpu
from jax.sharding import PartitionSpec as P

MESH = pl.DeviceIdType.MESH
F32, BF16 = jnp.float32, jnp.bfloat16

beta_one = 0.9
beta_two = 0.95
step_count = 20
rate = 0.002
decay = 0.1
epsilon = 1e-08

NJ = 4
TOK = 512
FEAT = 1024
HALF = 512


def schedule():
    order = []

    def add(stage, j, x=0):
        if 0 <= j < NJ:
            order.append((stage, j, x))

    for i in range(NJ + 1):
        add("g2", i - 1, 1)
        add("g0", i, 0)
        add("wc", i - 2, 1)
        add("g3", i - 1, 1)
        add("gx", i - 1)
        add("g1", i, 0)
        add("wd", i - 2, 0)
        add("wd", i - 2, 1)
        add("gy", i - 1)
        add("g2", i, 0)
        add("g0", i, 1)
        add("wa", i - 1, 1)
        add("wb", i - 1, 0)
        add("g1", i, 1)
        add("wb", i - 1, 1)
        add("g3", i, 0)
        add("wc", i - 1, 0)
        add("gg", i - 1)
    j = NJ - 1
    return order + [("wc", j, 1), ("wd", j, 0), ("wd", j, 1), ("last", 0, 0)]


def adamw(master, moment_one, moment_two, grad):
    first = beta_one * moment_one + (1.0 - beta_one) * grad
    second = beta_two * moment_two + (1.0 - beta_two) * grad * grad
    first_hat = first / (1.0 - beta_one**step_count)
    second_hat = second / (1.0 - beta_two**step_count)
    updated = master - rate * (first_hat / (jnp.sqrt(second_hat) + epsilon) + decay * master)
    return (updated, first, second)


def main_kernel(
    hid,
    lengths,
    kv,
    master,
    first,
    second,
    fresh_out,
    g_out,
    count_out,
    hbuf,
    cbuf,
    kvbuf,
    gbuf,
    r1,
    r2,
    r3,
    r4,
    wbuf,
    acc,
    fsend,
    frecv,
    mbuf,
    cnt,
    send_s,
    recv_s,
    gg_s,
    gg_r,
    h_s,
    h_r,
    h_l,
    small_s,
    small_r,
    load_s,
):
    y = lax.axis_index("rep")
    s = lax.axis_index("shard")
    t = lax.axis_index("tp")
    z = s // 4
    xl = (s // 2) % 2
    c = s % 2

    def ydev(d):
        return ((y + d) % 4, s, t)

    def zdev(d):
        return (y, ((z + d) % 4) * 4 + s % 4, t)

    xdev = (y, z * 4 + (1 - xl) * 2 + c, t)
    sib = (y, z * 4 + xl * 2 + (1 - c), t)

    def partner(core):
        return (y, z * 4 + xl * 2 + core, 1 - t)

    peers = [ydev(1), ydev(2), ydev(3), zdev(1), zdev(2), zdev(3), xdev, sib, partner(0), partner(1)]
    sends = []

    def put(src, dst, ss, rs, dev):
        copy = pltpu.make_async_remote_copy(src, dst, ss, rs, device_id=dev, device_id_type=MESH)
        copy.start()
        sends.append(copy)

    def got(dst, rs):
        pltpu.make_async_remote_copy(dst, dst, rs, rs, device_id=sib, device_id_type=MESH).wait_recv()

    mine = pl.ds(pl.multiple_of(c * 512 + t * 256, 256), 256)

    def columns(j, x, n, core):
        return pl.ds(pl.multiple_of((4 * n + 2 * x + core) * 512 + j * 128, 128), 128)

    def lanes(n):
        return pl.ds(pl.multiple_of(n * 128, 128), 128)

    def h_local(j, x):
        @pl.loop(0, 4)
        def _(n):
            pltpu.make_async_copy(
                hid.at[:, columns(j, x, n, c)], hbuf.at[j, x, mine, lanes(n)], h_l.at[j, x]
            ).start()

    def h_send(j, x):
        for k, (dev, core) in enumerate(((partner(0), 0), (partner(1), 1), (sib, 1 - c))):

            @pl.loop(0, 4)
            def _(n):
                pltpu.make_async_remote_copy(
                    hid.at[:, columns(j, x, n, core)],
                    hbuf.at[j, x, mine, lanes(n)],
                    h_s.at[j, x, k],
                    h_r.at[j, x, c * 2 + t],
                    device_id=dev,
                    device_id_type=MESH,
                ).start()

    def h_wait(j, x):
        pltpu.make_async_copy(hbuf.at[j, x, mine], hbuf.at[j, x, mine], h_l.at[j, x]).wait()
        for core, tp in ((1 - c, t), (0, 1 - t), (1, 1 - t)):
            rows = pl.ds(pl.multiple_of(core * 512 + tp * 256, 256), 256)
            got(hbuf.at[j, x, rows], h_r.at[j, x, core * 2 + tp])

    barrier = pltpu.get_barrier_semaphore()
    for dev in peers:
        pl.semaphore_signal(barrier, inc=1, device_id=dev, device_id_type=MESH)
    pl.semaphore_wait(barrier, len(peers))

    h_send(0, 0)

    kv_load = pltpu.make_async_copy(kv, kvbuf, load_s.at[3])
    kv_load.start()
    for m in range(2 * NJ):
        h_local(m // 2, m % 2)
    loads = []
    for k, ref in enumerate((master, first, second)):
        for j in range(NJ):
            loads.append(
                pltpu.make_async_copy(
                    ref.at[pl.ds(j * 128 + y * 32, 32)], mbuf.at[k, j], load_s.at[4 + k * NJ + j]
                )
            )
    for load in loads:
        load.start()

    def count_step(base, n, me, devs, sem):
        for d in range(1, n):
            put(cnt.at[base + me], cnt.at[base + me], small_s.at[sem + d], small_r.at[sem + d], devs(d))

    def count_sum(base, n, me, sem):
        for d in range(1, n):
            got(cnt.at[base + (me + n - d) % n], small_r.at[sem + d])
        total = cnt[base]
        for d in range(1, n):
            total = total + cnt[base + d]
        return total

    cnt[y] = jnp.full((8, 128), lengths[0], jnp.int32).astype(F32)
    count_step(0, 4, y, ydev, 0)

    kv_load.wait()

    @pl.loop(0, 8)
    def _(b):
        rows = pl.ds(pl.multiple_of(b * 64, 64), 64)
        value = kvbuf[rows].astype(F32)
        token = lax.broadcasted_iota(jnp.int32, (64, 8, 128), 0) + b * 64
        value = jnp.where(token < lengths[0], value, 0.0)
        cbuf[pl.ds(pl.multiple_of(c * 512 + b * 64, 64), 64)] = value.reshape(64, FEAT).astype(BF16)

    own_c = cbuf.at[pl.ds(pl.multiple_of(c * 512, 512), 512)]
    sib_c = cbuf.at[pl.ds(pl.multiple_of((1 - c) * 512, 512), 512)]
    put(own_c, own_c, small_s.at[0], small_r.at[0], sib)

    cnt[4 + z] = count_sum(0, 4, y, 0)
    count_step(4, 4, z, zdev, 4)
    cnt[8 + xl] = count_sum(4, 4, z, 4)
    count_step(8, 2, xl, lambda d: xdev, 8)
    cnt[10 + c] = count_sum(8, 2, xl, 8)
    count_step(10, 2, c, lambda d: sib, 10)
    count_out[...] = count_sum(10, 2, c, 10)

    got(sib_c, small_r.at[0])

    index = ((y, z), (z, y))
    devs = ((ydev, zdev), (zdev, ydev))
    every = slice(None)
    LOW, HIGH = pl.ds(0, 2), pl.ds(2, 2)

    def at(j, x, h, a1, a2=every):
        return (j, x, h, a2, a1) if h == 0 else (j, x, h, a1, a2)

    def g0(j, x):
        h_wait(j, x)
        m = 2 * j + x
        for ahead in (m + 1,):
            if ahead < 2 * NJ:
                h_send(ahead // 2, ahead % 2)

        @pl.loop(0, 2)
        def _(n):
            left = hbuf[j, x, :, pl.ds(pl.multiple_of(n * 256, 256), 256)]
            pair = pl.ds(n * 2, 2)
            for h in range(2):
                part = lax.dot_general(
                    left,
                    cbuf[:, h * HALF : (h + 1) * HALF],
                    (((0,), (0,)), ((), ())),
                    preferred_element_type=F32,
                )
                gbuf[j, x, h, pair] = part.astype(BF16).reshape(2, 4, 32, HALF)

        for h in range(2):
            far = (index[h][0] + 2) % 4
            for k, (d, part) in enumerate(((1, LOW), (3, HIGH))):
                put(
                    gbuf.at[at(j, x, h, far, part)],
                    r1.at[j, x, h, k],
                    send_s.at[j, x, h, k],
                    recv_s.at[j, x, h, k],
                    devs[h][0](d),
                )

    def g1(j, x):
        for h in range(2):
            i1 = index[h][0]
            for k, (d, low) in enumerate(((1, 0), (3, 2))):
                got(r1.at[j, x, h, k], recv_s.at[j, x, h, k])
                to = (i1 + d) % 4
                for a in range(2):
                    spot = at(j, x, h, to, low + a)
                    gbuf[spot] = (gbuf[spot].astype(F32) + r1[j, x, h, k, a].astype(F32)).astype(BF16)
                put(
                    gbuf.at[at(j, x, h, to)],
                    r2.at[j, x, h, k],
                    send_s.at[j, x, h, 2 + k],
                    recv_s.at[j, x, h, 2 + k],
                    devs[h][0](d),
                )

    def g2(j, x):
        for h in range(2):
            i1, i2 = index[h]
            for k in range(2):
                got(r2.at[j, x, h, k], recv_s.at[j, x, h, 2 + k])
            for d in (2, 1, 3, 0):
                a2 = (i2 + d) % 4
                spot = at(j, x, h, i1, a2)
                gbuf[spot] = (
                    gbuf[spot].astype(F32) + r2[j, x, h, 0, a2].astype(F32) + r2[j, x, h, 1, a2].astype(F32)
                ).astype(BF16)
                if d:
                    put(
                        gbuf.at[spot],
                        r3.at[j, x, h, d - 1],
                        send_s.at[j, x, h, 3 + d],
                        recv_s.at[j, x, h, 3 + d],
                        devs[h][1](d),
                    )

    def g3(j, x):
        for h in range(2):
            i1, i2 = index[h]
            for d in range(1, 4):
                got(r3.at[j, x, h, d - 1], recv_s.at[j, x, h, 3 + d])
            spot = at(j, x, h, i1, i2)
            total = gbuf[spot].astype(F32)
            for d in range(3):
                total = total + r3[j, x, h, d].astype(F32)
            gbuf[spot] = total.astype(BF16)

    def gx(j):
        for h in range(2):
            put(gbuf.at[at(j, 1 - xl, h, *index[h])], r4.at[j, h], send_s.at[j, 0, h, 14], recv_s.at[j, 0, h, 14], xdev)

    def gy(j):
        for k in range(3):
            loads[k * NJ + j].wait()
        count = jnp.broadcast_to(count_out[0:1, 0:1], (32, FEAT))
        halves = []
        for h in range(2):
            got(r4.at[j, h], recv_s.at[j, 0, h, 14])
            halves.append(gbuf[at(j, xl, h, *index[h])].astype(F32) + r4[j, h].astype(F32))
        summed = jnp.concatenate(halves, axis=1).astype(BF16)
        g_out[j, y] = summed
        grad = summed.astype(F32) / count
        new, _, _ = adamw(*(mbuf[k, j].reshape(32, FEAT) for k in range(3)), grad)
        new = new.astype(BF16)
        for h in range(2):
            spot = at(j, xl, h, *index[h])
            wbuf[spot] = new[:, h * HALF : (h + 1) * HALF]
            own = wbuf.at[spot]
            put(own, own, send_s.at[j, 0, h, 15], recv_s.at[j, 0, h, 15], xdev)
        wa(j, 0)

    def gg(j):
        for d in range(1, 4):
            put(g_out.at[j, y], g_out.at[j, y], gg_s.at[j, d - 1], gg_r.at[j, d - 1], ydev(d))

    def side(k):
        return 1 - xl if k else xl

    def wa(j, k):
        for h in range(2):
            own = wbuf.at[at(j, side(k), h, *index[h])]
            if k:
                got(own, recv_s.at[j, 0, h, 15])
            for d in (2, 1, 3):
                put(own, own, send_s.at[j, k, h, 6 + d], recv_s.at[j, k, h, 6 + d], devs[h][1](d))

    def wb(j, k):
        for h in range(2):
            i1, i2 = index[h]
            for d in range(1, 4):
                got(wbuf.at[at(j, side(k), h, i1, (i2 + 4 - d) % 4)], recv_s.at[j, k, h, 6 + d])
            own = wbuf.at[at(j, side(k), h, i1)]
            for n, d in enumerate((1, 3)):
                put(own, own, send_s.at[j, k, h, 10 + n], recv_s.at[j, k, h, 10 + n], devs[h][0](d))

    def wc(j, k):
        for h in range(2):
            i1 = index[h][0]
            for n, (d, part) in enumerate(((1, LOW), (3, HIGH))):
                back = (i1 + 4 - d) % 4
                got(wbuf.at[at(j, side(k), h, back)], recv_s.at[j, k, h, 10 + n])
                piece = wbuf.at[at(j, side(k), h, back, part)]
                put(piece, piece, send_s.at[j, k, h, 12 + n], recv_s.at[j, k, h, 12 + n], devs[h][0](d))

    def wd(j, k):
        for h in range(2):
            far = (index[h][0] + 2) % 4
            for n, part in enumerate((LOW, HIGH)):
                got(wbuf.at[at(j, side(k), h, far, part)], recv_s.at[j, k, h, 12 + n])

        def times(rows, h):
            return jnp.dot(
                hbuf[j, side(k), rows], wbuf[j, side(k), h].reshape(512, HALF), preferred_element_type=F32
            )

        if (j, k) != (NJ - 1, 1):

            @pl.loop(0, 4)
            def _(b):
                rows = pl.ds(pl.multiple_of(b * 256, 256), 256)
                for h in range(2):
                    cols = slice(h * HALF, (h + 1) * HALF)
                    if (j, k) == (0, 0):
                        acc[rows, cols] = times(rows, h)
                    else:
                        acc[rows, cols] += times(rows, h)
        else:
            for b in range(4):
                core = 1 - c if b < 2 else c
                rows = pl.ds(pl.multiple_of(core * 512 + (b % 2) * 256, 256), 256)
                for h in range(2):
                    cols = slice(h * HALF, (h + 1) * HALF)
                    part = acc[rows, cols] + times(rows, h)
                    if b < 2:
                        fsend[b, :, cols] = part.astype(BF16)
                    else:
                        acc[rows, cols] = part
                if b < 2:
                    put(fsend.at[b], frecv.at[b], small_s.at[12 + b], small_r.at[12 + b], sib)

    def last():
        for b in range(2):
            got(frecv.at[b], small_r.at[12 + b])
            rows = pl.ds(pl.multiple_of(c * 512 + b * 256, 256), 256)
            fresh_out[b * 256 : (b + 1) * 256] = (acc[rows] + frecv[b].astype(F32)).astype(BF16)

    for stage, j, x in schedule():
        if stage == "g0":
            g0(j, x)
        elif stage == "g1":
            g1(j, x)
        elif stage == "g2":
            g2(j, x)
        elif stage == "g3":
            g3(j, x)
        elif stage == "gx":
            gx(j)
        elif stage == "gy":
            gy(j)
        elif stage == "gg":
            gg(j)
        elif stage == "wa":
            wa(j, x)
        elif stage == "wb":
            wb(j, x)
        elif stage == "wc":
            wc(j, x)
        elif stage == "wd":
            wd(j, x)
        else:
            last()

    for j in range(NJ):
        for d in range(1, 4):
            got(g_out.at[j, (y + 4 - d) % 4], gg_r.at[j, d - 1])
        for x in range(2):
            for k in range(3):
                whole = hbuf.at[j, x, mine]
                pltpu.make_async_remote_copy(
                    whole, whole, h_s.at[j, x, k], h_s.at[j, x, k], device_id=sib, device_id_type=MESH
                ).wait_send()
    for copy in sends:
        copy.wait_send()


def finish_kernel(g, count, master, first, second, fresh, new_master, new_first, new_second, fresh_out):
    rows = master.shape[0]
    summed = g[...].astype(F32).reshape(rows, 8, 128)
    grad = summed / jnp.broadcast_to(count[...][0:1, 0:1].reshape(1, 1, 1), (rows, 8, 128))
    a, b, d = adamw(master[...], first[...], second[...], grad)
    new_master[...] = a
    new_first[...] = b
    new_second[...] = d
    fresh_out[...] = fresh[...].astype(F32).reshape(rows, 8, 128).astype(BF16)


def tiles(array):
    n = array.shape[0]
    return array.reshape(n, 2, 4, 128).transpose(0, 2, 1, 3).reshape(n, 8, 128)


def untiles(array):
    n = array.shape[0]
    return array.reshape(n, 4, 2, 128).transpose(0, 2, 1, 3).reshape(n, 2, 512)


def local(hidden_in, lengths, kv_grad_out, master, moment_one, moment_two):
    kv = tiles(kv_grad_out)
    states = [tiles(a) for a in (master, moment_one, moment_two)]
    hbm = pl.BlockSpec(memory_space=pl.ANY)
    vmem = pl.BlockSpec(memory_space=pltpu.VMEM)
    dma = pltpu.SemaphoreType.DMA
    fresh, g, count = pl.pallas_call(
        main_kernel,
        out_shape=(
            jax.ShapeDtypeStruct((TOK, FEAT), BF16),
            jax.ShapeDtypeStruct((NJ, 4, 32, FEAT), BF16),
            jax.ShapeDtypeStruct((8, 128), F32),
        ),
        in_specs=[hbm, pl.BlockSpec(memory_space=pltpu.SMEM), hbm, hbm, hbm, hbm],
        out_specs=(vmem, vmem, vmem),
        scratch_shapes=[
            pltpu.VMEM((NJ, 2, 1024, 512), BF16),
            pltpu.VMEM((1024, FEAT), BF16),
            pltpu.VMEM((TOK, 8, 128), BF16),
            pltpu.VMEM((NJ, 2, 2, 4, 4, 32, HALF), BF16),
            pltpu.VMEM((NJ, 2, 2, 2, 2, 32, HALF), BF16),
            pltpu.VMEM((NJ, 2, 2, 2, 4, 32, HALF), BF16),
            pltpu.VMEM((NJ, 2, 2, 3, 32, HALF), BF16),
            pltpu.VMEM((NJ, 2, 32, HALF), BF16),
            pltpu.VMEM((NJ, 2, 2, 4, 4, 32, HALF), BF16),
            pltpu.VMEM((1024, FEAT), F32),
            pltpu.VMEM((2, 256, FEAT), BF16),
            pltpu.VMEM((2, 256, FEAT), BF16),
            pltpu.VMEM((3, NJ, 32, 8, 128), F32),
            pltpu.VMEM((12, 8, 128), F32),
            dma((NJ, 2, 2, 16)),
            dma((NJ, 2, 2, 16)),
            dma((NJ, 3)),
            dma((NJ, 3)),
            dma((NJ, 2, 3)),
            dma((NJ, 2, 4)),
            dma((NJ, 2)),
            dma((14,)),
            dma((14,)),
            dma((4 + 3 * NJ,)),
        ],
        compiler_params=pltpu.CompilerParams(
            collective_id=0, has_side_effects=True, vmem_limit_bytes=50 * 2**20
        ),
        name="project",
    )(hidden_in, lengths, kv, *states)
    g = g.reshape(TOK, FEAT)
    step = 64
    flat = pl.BlockSpec((step, FEAT), lambda i: (i, 0))
    cube = pl.BlockSpec((step, 8, 128), lambda i: (i, 0, 0))
    outs = pl.pallas_call(
        finish_kernel,
        grid=(TOK // step,),
        out_shape=[jax.ShapeDtypeStruct((TOK, 8, 128), F32)] * 3
        + [jax.ShapeDtypeStruct((TOK, 8, 128), BF16)],
        in_specs=[flat, pl.BlockSpec((8, 128), lambda i: (0, 0)), cube, cube, cube, flat],
        out_specs=[cube] * 4,
        compiler_params=pltpu.CompilerParams(vmem_limit_bytes=24 * 2**20),
        name="update",
    )(g, count, *states, fresh)
    return tuple(untiles(a) for a in outs)


def solution(mesh):
    in_specs = (
        P(("rep", "shard", "tp"), None),
        P(("rep", "shard")),
        P(("rep", "shard"), None, "tp"),
        P("shard", None, "tp"),
        P("shard", None, "tp"),
        P("shard", None, "tp"),
    )
    out_specs = (
        P("shard", None, "tp"),
        P("shard", None, "tp"),
        P("shard", None, "tp"),
        P(("rep", "shard"), None, "tp"),
    )
    return jax.shard_map(local, mesh=mesh, in_specs=in_specs, out_specs=out_specs, check_vma=False)
```

time: 219 us -> 178 us (0.81)
  Pallas kernels: 212 us -> 175 us
  local copies, waits for them, and re-layouts: 6.31 us -> 1.23 us
    pallas_call x1, Pallas kernels: 206 us -> 170 us  [local(): pl.pallas_call(main_kernel, out_shape=(jax.ShapeDtypeStruct((TOK, FEAT),...]
    unnamed x12 -> x8, local copies, waits for them, and re-layouts: 6.31 us -> 1.23 us
where the time goes in v2:
time: 178 us
  Pallas kernels  175 us (98%)
    pallas_call x1, Pallas kernels, local(): pl.pallas_call(main_kernel, out_shape=(jax.ShapeDtypeStruct((TOK, FEAT),...  170 us
    pallas_call x1, Pallas kernels, local(): pl.pallas_call(finish_kernel, grid=(TOK // step,), out_shape=[jax.ShapeDt...  5.32 us

profile of v2, /device:TPU:1, one launch (start us, length us, event | category | flops | bytes accessed | tf_op | source)
XLA Modules:
  0.0 177.8 jit_solution(827485623470867400)
XLA Ops:
  1.3 0.0 copy-start.3
  1.3 1.2 copy-done.3
  2.5 0.0 copy-start
  2.5 0.0 copy-start.1
  2.5 0.0 copy-start.2
  2.5 169.9 %project.1 = (bf16[512,1024]{1,0:T(8,128)(2,1)S(1)}, bf16[4,4,32,1024]{3,2,1,0:T(8,128)(2,1)S(1)}, f32[8,128]{1,0:T(8,128)S(1)}) custom-call(bf16[256,8192]{1,0:T(8,128)(2,1)} %hid.1, s32[1]{0:T(128)S(6)} %copy.18.lengths, bf16[512,8,128]{2,1,0:T(8,128)(2,1)S(1)} %bitcast.47, f32[512,8,128]{2,1,0:T(8,128)} %bitcast.41, f32[512,8,128]{2,1,0:T(8,128)} %bitcast.43, ...), custom_call_target="tpu_custom_call" | custom-call | tf_op jit(solution)/shard_map/project/pallas_call | solution.py:478
  172.4 0.0 copy-done
  172.4 0.0 copy-done.1
  172.4 0.0 copy-done.2
  172.4 5.3 %update.1 = (f32[512,8,128]{2,1,0:T(8,128)}, f32[512,8,128]{2,1,0:T(8,128)}, f32[512,8,128]{2,1,0:T(8,128)}, bf16[512,8,128]{2,1,0:T(8,128)(2,1)}) custom-call(bf16[512,1024]{1,0:T(8,128)(2,1)S(1)} %bitcast.48, f32[8,128]{1,0:T(8,128)S(1)} %get-tuple-element.12.count, f32[512,8,128]{2,1,0:T(8,128)S(1)} %bitcast.42, f32[512,8,128]{2,1,0:T(8,128)S(1)} %bitcast.44, ...), custom_call_target="tpu_custom_call" | custom-call | tf_op jit(solution)/shard_map/update/pallas_call | solution.py:522
Async XLA Ops:
  1.3 1.2 copy-start.3
  2.5 169.9 %copy-start = (f32[512,2,512]{2,1,0:T(2,128)S(1)}, f32[512,2,512]{2,1,0:T(2,128)}, u32[]{:S(2)}) copy-start(f32[512,2,512]{2,1,0:T(2,128)} %param.9) | copy-start | bytes 6291460
  2.5 169.9 %copy-start.1 = (f32[512,2,512]{2,1,0:T(2,128)S(1)}, f32[512,2,512]{2,1,0:T(2,128)}, u32[]{:S(2)}) copy-start(f32[512,2,512]{2,1,0:T(2,128)} %param.10) | copy-start | bytes 6291460
  2.5 169.9 %copy-start.2 = (f32[512,2,512]{2,1,0:T(2,128)S(1)}, f32[512,2,512]{2,1,0:T(2,128)}, u32[]{:S(2)}) copy-start(f32[512,2,512]{2,1,0:T(2,128)} %param.11) | copy-start | bytes 6291460

commit v3 on v2

--- a/solution.py
+++ b/solution.py
@@ -17,6 +17,7 @@
 decay = 0.1
 epsilon = 1e-08
 
+AHEAD = 7
 NJ = 4
 TOK = 512
 FEAT = 1024
@@ -29,26 +30,38 @@
     def add(stage, j, x=0):
         if 0 <= j < NJ:
             order.append((stage, j, x))
+
+    def send(m, n):
+        if m < 2 * NJ:
+            order.append(("h", 4 * m + n + AHEAD, 0))
 
     for i in range(NJ + 1):
         add("g2", i - 1, 1)
         add("g0", i, 0)
         add("wc", i - 2, 1)
         add("g3", i - 1, 1)
-        add("gx", i - 1)
+        add("gx", i - 1, 0)
+        send(2 * i, 1)
         add("g1", i, 0)
         add("wd", i - 2, 0)
+        send(2 * i, 2)
         add("wd", i - 2, 1)
-        add("gy", i - 1)
+        add("gy", i - 1, 0)
+        add("gg", i - 1, 0)
         add("g2", i, 0)
+        send(2 * i, 3)
         add("g0", i, 1)
         add("wa", i - 1, 1)
         add("wb", i - 1, 0)
+        send(2 * i + 1, 1)
         add("g1", i, 1)
+        add("g3", i, 0)
+        send(2 * i + 1, 2)
         add("wb", i - 1, 1)
-        add("g3", i, 0)
         add("wc", i - 1, 0)
-        add("gg", i - 1)
+        send(2 * i + 1, 3)
+    for n in range(4):
+        order.insert(order.index(("g%d" % min(n, 3), 0, 0 if n < 3 else 1)) + 1, ("count", 0, n))
     j = NJ - 1
     return order + [("wc", j, 1), ("wd", j, 0), ("wd", j, 1), ("last", 0, 0)]
 
@@ -56,8 +69,8 @@
 def adamw(master, moment_one, moment_two, grad):
     first = beta_one * moment_one + (1.0 - beta_one) * grad
     second = beta_two * moment_two + (1.0 - beta_two) * grad * grad
-    first_hat = first / (1.0 - beta_one**step_count)
-    second_hat = second / (1.0 - beta_two**step_count)
+    first_hat = first * (1.0 / (1.0 - beta_one**step_count))
+    second_hat = second * (1.0 / (1.0 - beta_two**step_count))
     updated = master - rate * (first_hat / (jnp.sqrt(second_hat) + epsilon) + decay * master)
     return (updated, first, second)
 
@@ -142,19 +155,20 @@
                 hid.at[:, columns(j, x, n, c)], hbuf.at[j, x, mine, lanes(n)], h_l.at[j, x]
             ).start()
 
-    def h_send(j, x):
+    def h_send(quarter):
+        m, n = divmod(quarter, 4)
+        if m >= 2 * NJ:
+            return
+        j, x = divmod(m, 2)
         for k, (dev, core) in enumerate(((partner(0), 0), (partner(1), 1), (sib, 1 - c))):
-
-            @pl.loop(0, 4)
-            def _(n):
-                pltpu.make_async_remote_copy(
-                    hid.at[:, columns(j, x, n, core)],
-                    hbuf.at[j, x, mine, lanes(n)],
-                    h_s.at[j, x, k],
-                    h_r.at[j, x, c * 2 + t],
-                    device_id=dev,
-                    device_id_type=MESH,
-                ).start()
+            pltpu.make_async_remote_copy(
+                hid.at[:, columns(j, x, n, core)],
+                hbuf.at[j, x, mine, lanes(n)],
+                h_s.at[j, x, k],
+                h_r.at[j, x, c * 2 + t],
+                device_id=dev,
+                device_id_type=MESH,
+            ).start()
 
     def h_wait(j, x):
         pltpu.make_async_copy(hbuf.at[j, x, mine], hbuf.at[j, x, mine], h_l.at[j, x]).wait()
@@ -167,7 +181,8 @@
         pl.semaphore_signal(barrier, inc=1, device_id=dev, device_id_type=MESH)
     pl.semaphore_wait(barrier, len(peers))
 
-    h_send(0, 0)
+    for quarter in range(4):
+        h_send(quarter)
 
     kv_load = pltpu.make_async_copy(kv, kvbuf, load_s.at[3])
     kv_load.start()
@@ -213,14 +228,8 @@
     sib_c = cbuf.at[pl.ds(pl.multiple_of((1 - c) * 512, 512), 512)]
     put(own_c, own_c, small_s.at[0], small_r.at[0], sib)
 
-    cnt[4 + z] = count_sum(0, 4, y, 0)
-    count_step(4, 4, z, zdev, 4)
-    cnt[8 + xl] = count_sum(4, 4, z, 4)
-    count_step(8, 2, xl, lambda d: xdev, 8)
-    cnt[10 + c] = count_sum(8, 2, xl, 8)
-    count_step(10, 2, c, lambda d: sib, 10)
-    count_out[...] = count_sum(10, 2, c, 10)
-
+    for quarter in range(4, AHEAD):
+        h_send(quarter)
     got(sib_c, small_r.at[0])
 
     index = ((y, z), (z, y))
@@ -233,10 +242,7 @@
 
     def g0(j, x):
         h_wait(j, x)
-        m = 2 * j + x
-        for ahead in (m + 1,):
-            if ahead < 2 * NJ:
-                h_send(ahead // 2, ahead % 2)
+        h_send(8 * j + 4 * x + AHEAD)
 
         @pl.loop(0, 2)
         def _(n):
@@ -317,14 +323,14 @@
     def gy(j):
         for k in range(3):
             loads[k * NJ + j].wait()
-        count = jnp.broadcast_to(count_out[0:1, 0:1], (32, FEAT))
+        inverse = jnp.broadcast_to(1.0 / count_out[0:1, 0:1], (32, FEAT))
         halves = []
         for h in range(2):
             got(r4.at[j, h], recv_s.at[j, 0, h, 14])
             halves.append(gbuf[at(j, xl, h, *index[h])].astype(F32) + r4[j, h].astype(F32))
         summed = jnp.concatenate(halves, axis=1).astype(BF16)
         g_out[j, y] = summed
-        grad = summed.astype(F32) / count
+        grad = summed.astype(F32) * inverse
         new, _, _ = adamw(*(mbuf[k, j].reshape(32, FEAT) for k in range(3)), grad)
         new = new.astype(BF16)
         for h in range(2):
@@ -408,6 +414,19 @@
             got(frecv.at[b], small_r.at[12 + b])
             rows = pl.ds(pl.multiple_of(c * 512 + b * 256, 256), 256)
             fresh_out[b * 256 : (b + 1) * 256] = (acc[rows] + frecv[b].astype(F32)).astype(BF16)
+
+    def count_stage(n):
+        if n == 0:
+            cnt[4 + z] = count_sum(0, 4, y, 0)
+            count_step(4, 4, z, zdev, 4)
+        elif n == 1:
+            cnt[8 + xl] = count_sum(4, 4, z, 4)
+            count_step(8, 2, xl, lambda d: xdev, 8)
+        elif n == 2:
+            cnt[10 + c] = count_sum(8, 2, xl, 8)
+            count_step(10, 2, c, lambda d: sib, 10)
+        else:
+            count_out[...] = count_sum(10, 2, c, 10)
 
     for stage, j, x in schedule():
         if stage == "g0":
@@ -432,6 +451,10 @@
             wc(j, x)
         elif stage == "wd":
             wd(j, x)
+        elif stage == "h":
+            h_send(j)
+        elif stage == "count":
+            count_stage(x)
         else:
             last()
 
@@ -451,7 +474,7 @@
 def finish_kernel(g, count, master, first, second, fresh, new_master, new_first, new_second, fresh_out):
     rows = master.shape[0]
     summed = g[...].astype(F32).reshape(rows, 8, 128)
-    grad = summed / jnp.broadcast_to(count[...][0:1, 0:1].reshape(1, 1, 1), (rows, 8, 128))
+    grad = summed * jnp.broadcast_to((1.0 / count[...])[0:1, 0:1].reshape(1, 1, 1), (rows, 8, 128))
     a, b, d = adamw(master[...], first[...], second[...], grad)
     new_master[...] = a
     new_first[...] = b
@@ -482,7 +505,7 @@
             jax.ShapeDtypeStruct((NJ, 4, 32, FEAT), BF16),
             jax.ShapeDtypeStruct((8, 128), F32),
         ),
-        in_specs=[hbm, pl.BlockSpec(memory_space=pltpu.SMEM), hbm, hbm, hbm, hbm],
+        in_specs=[hbm, pl.BlockSpec(memory_space=pltpu.SMEM), pl.BlockSpec(memory_space=pltpu.HBM), hbm, hbm, hbm],
         out_specs=(vmem, vmem, vmem),
         scratch_shapes=[
             pltpu.VMEM((NJ, 2, 1024, 512), BF16),

time: 178 us -> 170 us (0.955)
  Pallas kernels: 175 us -> 168 us
    pallas_call x1, Pallas kernels: 170 us -> 162 us  [local(): pl.pallas_call(main_kernel, out_shape=(jax.ShapeDtypeStruct((TOK, FEAT),...]
where the time goes in v3:
time: 170 us
  Pallas kernels  168 us (99%)
    pallas_call x1, Pallas kernels, local(): pl.pallas_call(main_kernel, out_shape=(jax.ShapeDtypeStruct((TOK, FEAT),...  162 us
    pallas_call x1, Pallas kernels, local(): pl.pallas_call(finish_kernel, grid=(TOK // step,), out_shape=[jax.ShapeDt...  5.34 us

profile of v3, /device:TPU:1, one launch (start us, length us, event | category | flops | bytes accessed | tf_op | source)
XLA Modules:
  0.0 170.1 jit_solution(8284477509653636532)
XLA Ops:
  1.3 0.0 copy-start.3
  1.3 1.2 copy-done.3
  2.5 0.0 copy-start
  2.5 0.0 copy-start.1
  2.5 0.0 copy-start.2
  2.5 162.2 %project.1 = (bf16[512,1024]{1,0:T(8,128)(2,1)S(1)}, bf16[4,4,32,1024]{3,2,1,0:T(8,128)(2,1)S(1)}, f32[8,128]{1,0:T(8,128)S(1)}) custom-call(bf16[256,8192]{1,0:T(8,128)(2,1)} %hid.1, s32[1]{0:T(128)S(6)} %copy.18.lengths, bf16[512,8,128]{2,1,0:T(8,128)(2,1)S(1)} %bitcast.47, f32[512,8,128]{2,1,0:T(8,128)} %bitcast.41, f32[512,8,128]{2,1,0:T(8,128)} %bitcast.43, ...), custom_call_target="tpu_custom_call" | custom-call | tf_op jit(solution)/shard_map/project/pallas_call | solution.py:501
  164.7 0.0 copy-done
  164.7 0.0 copy-done.1
  164.7 0.0 copy-done.2
  164.7 5.3 %update.1 = (f32[512,8,128]{2,1,0:T(8,128)}, f32[512,8,128]{2,1,0:T(8,128)}, f32[512,8,128]{2,1,0:T(8,128)}, bf16[512,8,128]{2,1,0:T(8,128)(2,1)}) custom-call(bf16[512,1024]{1,0:T(8,128)(2,1)S(1)} %bitcast.48, f32[8,128]{1,0:T(8,128)S(1)} %get-tuple-element.12.count, f32[512,8,128]{2,1,0:T(8,128)S(1)} %bitcast.42, f32[512,8,128]{2,1,0:T(8,128)S(1)} %bitcast.44, ...), custom_call_target="tpu_custom_call" | custom-call | tf_op jit(solution)/shard_map/update/pallas_call | solution.py:545
Async XLA Ops:
  1.3 1.2 copy-start.3
  2.5 162.2 %copy-start = (f32[512,2,512]{2,1,0:T(2,128)S(1)}, f32[512,2,512]{2,1,0:T(2,128)}, u32[]{:S(2)}) copy-start(f32[512,2,512]{2,1,0:T(2,128)} %param.9) | copy-start | bytes 6291460
  2.5 162.2 %copy-start.1 = (f32[512,2,512]{2,1,0:T(2,128)S(1)}, f32[512,2,512]{2,1,0:T(2,128)}, u32[]{:S(2)}) copy-start(f32[512,2,512]{2,1,0:T(2,128)} %param.10) | copy-start | bytes 6291460
  2.5 162.2 %copy-start.2 = (f32[512,2,512]{2,1,0:T(2,128)S(1)}, f32[512,2,512]{2,1,0:T(2,128)}, u32[]{:S(2)}) copy-start(f32[512,2,512]{2,1,0:T(2,128)} %param.11) | copy-start | bytes 6291460

commit v4 on v3

--- a/solution.py
+++ b/solution.py
@@ -45,12 +45,12 @@
         add("g1", i, 0)
         add("wd", i - 2, 0)
         send(2 * i, 2)
-        add("wd", i - 2, 1)
         add("gy", i - 1, 0)
         add("gg", i - 1, 0)
         add("g2", i, 0)
         send(2 * i, 3)
         add("g0", i, 1)
+        add("wd", i - 2, 1)
         add("wa", i - 1, 1)
         add("wb", i - 1, 0)
         send(2 * i + 1, 1)

time: 170 us -> 168 us (0.988)
  Pallas kernels: 168 us -> 165 us
    pallas_call x1, Pallas kernels: 162 us -> 160 us  [local(): pl.pallas_call(main_kernel, out_shape=(jax.ShapeDtypeStruct((TOK, FEAT),...]
where the time goes in v4:
time: 168 us
  Pallas kernels  165 us (98%)
    pallas_call x1, Pallas kernels, local(): pl.pallas_call(main_kernel, out_shape=(jax.ShapeDtypeStruct((TOK, FEAT),...  160 us
    pallas_call x1, Pallas kernels, local(): pl.pallas_call(finish_kernel, grid=(TOK // step,), out_shape=[jax.ShapeDt...  5.34 us

profile of v4, /device:TPU:1, one launch (start us, length us, event | category | flops | bytes accessed | tf_op | source)
XLA Modules:
  0.0 167.7 jit_solution(8479378620095031028)
XLA Ops:
  1.3 0.0 copy-start.3
  1.3 1.2 copy-done.3
  2.5 0.0 copy-start
  2.5 0.0 copy-start.1
  2.5 0.0 copy-start.2
  2.5 159.8 %project.1 = (bf16[512,1024]{1,0:T(8,128)(2,1)S(1)}, bf16[4,4,32,1024]{3,2,1,0:T(8,128)(2,1)S(1)}, f32[8,128]{1,0:T(8,128)S(1)}) custom-call(bf16[256,8192]{1,0:T(8,128)(2,1)} %hid.1, s32[1]{0:T(128)S(6)} %copy.18.lengths, bf16[512,8,128]{2,1,0:T(8,128)(2,1)S(1)} %bitcast.47, f32[512,8,128]{2,1,0:T(8,128)} %bitcast.41, f32[512,8,128]{2,1,0:T(8,128)} %bitcast.43, ...), custom_call_target="tpu_custom_call" | custom-call | tf_op jit(solution)/shard_map/project/pallas_call | solution.py:501
  162.3 0.0 copy-done
  162.3 0.0 copy-done.1
  162.3 0.0 copy-done.2
  162.3 5.3 %update.1 = (f32[512,8,128]{2,1,0:T(8,128)}, f32[512,8,128]{2,1,0:T(8,128)}, f32[512,8,128]{2,1,0:T(8,128)}, bf16[512,8,128]{2,1,0:T(8,128)(2,1)}) custom-call(bf16[512,1024]{1,0:T(8,128)(2,1)S(1)} %bitcast.48, f32[8,128]{1,0:T(8,128)S(1)} %get-tuple-element.12.count, f32[512,8,128]{2,1,0:T(8,128)S(1)} %bitcast.42, f32[512,8,128]{2,1,0:T(8,128)S(1)} %bitcast.44, ...), custom_call_target="tpu_custom_call" | custom-call | tf_op jit(solution)/shard_map/update/pallas_call | solution.py:545
Async XLA Ops:
  1.3 1.2 copy-start.3
  2.5 159.8 %copy-start = (f32[512,2,512]{2,1,0:T(2,128)S(1)}, f32[512,2,512]{2,1,0:T(2,128)}, u32[]{:S(2)}) copy-start(f32[512,2,512]{2,1,0:T(2,128)} %param.9) | copy-start | bytes 6291460
  2.5 159.8 %copy-start.1 = (f32[512,2,512]{2,1,0:T(2,128)S(1)}, f32[512,2,512]{2,1,0:T(2,128)}, u32[]{:S(2)}) copy-start(f32[512,2,512]{2,1,0:T(2,128)} %param.10) | copy-start | bytes 6291460
  2.5 159.8 %copy-start.2 = (f32[512,2,512]{2,1,0:T(2,128)S(1)}, f32[512,2,512]{2,1,0:T(2,128)}, u32[]{:S(2)}) copy-start(f32[512,2,512]{2,1,0:T(2,128)} %param.11) | copy-start | bytes 6291460
